TPU v7x, 32 devices: a whole 2x2x4 slice. The times are simulated.
32 devices in a mesh: outer: 8 (over z, y), inner: 4 (over x, core).
Axes of the slice: x: 2, y: 2, z: 4, core: 2. Of those that a mesh axis runs over, the one named last changes fastest.
Arguments:
- query_states: bfloat16 [4096, 4096], P(('outer', 'inner')), may hold values from -6 to 6
- key_states: bfloat16 [4096, 4096], P(('outer', 'inner')), may hold values from -6 to 6
- value_states: bfloat16 [4096, 4096], P(('outer', 'inner')), may hold values from -6 to 6
- doc_lengths: int32 [8], replicated, may hold values from 1 to 1024, 4096 in all
- slopes: float32 [32], replicated, may hold values from 0.00024414062 to 0.0625
Outputs:
- attended: bfloat16 [4096, 4096], P(('outer', 'inner'))
Inputs may be any that keep to these rules, and one draw needn't show every extreme that they name: `doc_lengths`: the lengths add up to 4096; the longest is exactly 1024.
All inputs are finite; a program needn't handle non-finite values.
Results may differ from a plain program's by a relative error of at most 0.0045.
Values may be sent and summed in bfloat16 or wider, within the bound.
A program may use at most 64 MiB of HBM per device.

v0:
```python
import math

import jax
import jax.numpy as jnp
from jax import lax
from jax.sharding import PartitionSpec as P

SPAN = 2


NEG_FILL = -1e30


def shifted(value, axis, steps):
    count = lax.axis_size(axis)
    first, last = (max(0, -steps), min(count, count - steps))
    return lax.ppermute(value, axis, [(source, source + steps) for source in range(first, last)])


def document_of(positions, doc_lengths):
    boundary = jnp.cumsum(doc_lengths)
    return jnp.sum((boundary[None, :] <= positions[:, None]).astype(jnp.int32), axis=1)


def empty_status(row_count, head_count, head_width):
    return (
        jnp.full((row_count, head_count), NEG_FILL, jnp.float32),
        jnp.zeros((row_count, head_count), jnp.float32),
        jnp.zeros((row_count, head_count, head_width), jnp.float32),
    )


def attend_block(status, query_parts, key_slab, value_slab, key_pos, key_doc, slopes):
    query_rows, query_pos, query_doc = query_parts
    allowed = (query_doc[:, None] == key_doc[None, :]) & (key_pos[None, :] <= query_pos[:, None])

    def update(current):
        running_max, row_total, weighted_sum = current
        scores = jnp.einsum(
            "qhd,khd->qhk", query_rows, key_slab, preferred_element_type=jnp.float32
        )
        scores = scores * (1.0 / math.sqrt(query_rows.shape[-1]))
        distance = (query_pos[:, None] - key_pos[None, :]).astype(jnp.float32)
        scores = scores - slopes[None, :, None] * distance[:, None, :]
        scores = jnp.where(allowed[:, None, :], scores, NEG_FILL)
        new_max = jnp.maximum(running_max, jnp.max(scores, axis=-1))
        weights = jnp.where(allowed[:, None, :], jnp.exp(scores - new_max[:, :, None]), 0.0)
        rescale = jnp.exp(running_max - new_max)
        row_total = row_total * rescale + jnp.sum(weights, axis=-1)
        products = jnp.einsum(
            "qhk,khd->qhd",
            weights.astype(jnp.bfloat16),
            value_slab,
            preferred_element_type=jnp.float32,
        )
        weighted_sum = weighted_sum * rescale[:, :, None] + products
        return (new_max, row_total, weighted_sum)

    def unchanged(current):
        return current

    return lax.cond(jnp.any(allowed), update, unchanged, status)


def attend_keys(status, query_parts, key_slab, value_slab, key_pos, slopes, doc_lengths):
    key_doc = document_of(key_pos, doc_lengths)
    key_count = key_slab.shape[0]
    slab_rows = 256
    pieces = key_count // slab_rows
    stacked = (
        key_slab.reshape((pieces, slab_rows) + key_slab.shape[1:]),
        value_slab.reshape((pieces, slab_rows) + value_slab.shape[1:]),
        key_pos.reshape(pieces, slab_rows),
        key_doc.reshape(pieces, slab_rows),
    )

    def scan_step(current, portion):
        return (
            attend_block(
                current, query_parts, portion[0], portion[1], portion[2], portion[3], slopes
            ),
            None,
        )

    result, unused = lax.scan(scan_step, status, stacked)
    return result


def combine(first_status, second_status):
    new_max = jnp.maximum(first_status[0], second_status[0])
    left_scale = jnp.exp(first_status[0] - new_max)
    right_scale = jnp.exp(second_status[0] - new_max)
    return (
        new_max,
        first_status[1] * left_scale + second_status[1] * right_scale,
        first_status[2] * left_scale[:, :, None] + second_status[2] * right_scale[:, :, None],
    )


def queries_from_later(query_rows, hops_back):
    return shifted(query_rows, "outer", -hops_back)


def partials_home(status, hops_back):
    running_max, row_total, weighted_sum = status
    moved_max, moved_total, moved_sum = shifted(
        (running_max, row_total, weighted_sum), "outer", hops_back
    )
    return (jnp.where(moved_total > 0.0, moved_max, NEG_FILL), moved_total, moved_sum)


def rows_of(status, slot_index, row_count):
    return tuple(
        (member[slot_index * row_count : (slot_index + 1) * row_count] for member in status)
    )


def bring_home(status, row_count, span_count):
    own_status = rows_of(status, 0, row_count)
    distant = [rows_of(status, hops_back, row_count) for hops_back in range(1, span_count + 1)]
    merged = own_status
    for hops_back in range(1, span_count + 1):
        merged = combine(merged, partials_home(distant[hops_back - 1], hops_back))
    return merged


def with_later_queries(own_rows, own_pos, group_rows, span_count, doc_lengths):
    rows_list = [own_rows]
    pos_list = [own_pos]
    for hops_back in range(1, span_count + 1):
        rows_list.append(queries_from_later(own_rows, hops_back))
        pos_list.append(own_pos + hops_back * group_rows)
    all_pos = jnp.concatenate(pos_list)
    return (jnp.concatenate(rows_list, axis=0), all_pos, document_of(all_pos, doc_lengths))


def normalize(status):
    return (status[2] / status[1][:, :, None]).astype(jnp.bfloat16)


def per_device(query_states, key_states, value_states, doc_lengths, slopes):
    rows_dev = query_states.shape[0]
    head_count = slopes.shape[0]
    head_width = query_states.shape[1] // head_count
    inner_count = lax.axis_size("inner")
    group_index = lax.axis_index("outer")
    inner_index = lax.axis_index("inner")
    group_rows = rows_dev * inner_count
    group_start = group_index * group_rows
    own_queries = query_states.reshape(rows_dev, head_count, head_width)
    own_pos = group_start + inner_index * rows_dev + jnp.arange(rows_dev, dtype=jnp.int32)
    query_parts = with_later_queries(own_queries, own_pos, group_rows, SPAN, doc_lengths)
    status = empty_status(query_parts[0].shape[0], head_count, head_width)
    portions = (
        lax.all_gather(
            key_states.reshape(rows_dev, head_count, head_width), "inner", axis=0, tiled=True
        ),
        lax.all_gather(
            value_states.reshape(rows_dev, head_count, head_width), "inner", axis=0, tiled=True
        ),
    )
    key_pos = group_start + jnp.arange(portions[0].shape[0], dtype=jnp.int32)
    status = attend_keys(
        status, query_parts, portions[0], portions[1], key_pos, slopes, doc_lengths
    )
    combined = bring_home(status, rows_dev, SPAN)
    return normalize(combined).reshape(rows_dev, head_count * head_width)


def solution(mesh):
    placed = (
        P(("outer", "inner"), None),
        P(("outer", "inner"), None),
        P(("outer", "inner"), None),
        P(),
        P(),
    )
    return jax.shard_map(
        per_device,
        mesh=mesh,
        in_specs=placed,
        out_specs=P(("outer", "inner"), None),
        check_vma=False,
    )
```

profile of v0, /device:TPU:0, one launch (start us, length us, event | category | flops | bytes accessed | tf_op | source)
XLA Modules:
  0.0 250.7 jit_solution(16918272236634218181)
XLA Ops:
  6.5 2.5 %copy.28 = bf16[16,8,32,128]{3,2,1,0:T(8,128)(2,1)} copy(bf16[16,8,32,128]{3,1,2,0:T(8,128)(2,1)} %bitcast.53) | data formatting | bytes 2097152
  9.1 0.0 all-gather.3.cloned.1.call-update
  9.1 0.0 all-gather.5.cloned.1.call-start
  9.1 2.4 copy.29
  11.6 0.0 all-gather.5.cloned.1.call-update
  11.6 0.7 copy.21
  12.3 1.3 collective-permute-start
  13.6 1.3 collective-permute-start.1
  14.9 0.2 reduce-window.8
  15.1 0.1 convert_reduce_fusion
  15.2 0.1 convert_reduce_fusion.1
  15.3 25.0 %collective-permute-done = bf16[128,32,128]{0,2,1:T(8,128)(2,1)S(1)} collective-permute-done((bf16[128,32,128]{0,2,1:T(8,128)(2,1)S(1)}, bf16[128,32,128]{0,2,1:T(8,128)(2,1)S(1)}, u32[]{:S(2)}, u32[]{:S(2)}) %collective-permute-start) | collective-permute-done | bytes 1048608 | tf_op jit(solution)/shard_map/ppermute | solution.py:17
  40.3 1.0 copy-done.4
  41.4 22.7 %collective-permute-done.1 = bf16[128,32,128]{0,2,1:T(8,128)(2,1)} collective-permute-done((bf16[128,32,128]{0,2,1:T(8,128)(2,1)S(1)}, bf16[128,32,128]{0,2,1:T(8,128)(2,1)}, u32[]{:S(2)}, u32[]{:S(2)}) %collective-permute-start.1) | collective-permute-done | bytes 1048608 | tf_op jit(solution)/shard_map/ppermute | solution.py:17
  64.1 2.4 pad_maximum_fusion
  66.4 2.9 %copy.23 = bf16[384,32,128]{2,0,1:T(8,128)(2,1)} copy(bf16[384,32,128]{0,2,1:T(8,128)(2,1)S(1)} %pad_maximum_fusion) | data formatting | bytes 6291456 | tf_op jit(solution)/shard_map/while | solution.py:85
  69.3 5.9 %copy.22 = bf16[2,256,32,128]{3,1,2,0:T(8,128)(2,1)} copy(bf16[2,256,32,128]{3,2,1,0:T(8,128)(2,1)} %bitcast.46) | data formatting | bytes 8388608 | tf_op jit(solution)/shard_map/while | solution.py:85
  75.2 7.3 %all-gather.5.cloned.1.call-done = bf16[512,32,128]{2,1,0:T(8,128)(2,1)} async-done(((bf16[128,32,128]{2,1,0:T(8,128)(2,1)}), bf16[512,32,128]{2,1,0:T(8,128)(2,1)}) %all-gather.5.cloned.1.call-update) | async-done | bytes 4194320 | tf_op jit(solution)/shard_map/all_gather | solution.py:158
  82.5 6.0 %copy.24 = bf16[2,256,32,128]{3,1,2,0:T(8,128)(2,1)} copy(bf16[2,256,32,128]{3,2,1,0:T(8,128)(2,1)} %bitcast.47) | data formatting | bytes 8388608 | tf_op jit(solution)/shard_map/while | solution.py:85
  88.5 3.4 %broadcast_in_dim.61 = f32[384,32,128]{2,0,1:T(8,128)} broadcast(f32[]{:T(128)} %constant.59.clone.1), dimensions={} | broadcast | bytes 6291460 | tf_op jit(solution)/shard_map/broadcast_in_dim | solution.py:29
  92.0 41.3 %while.14 = (s32[]{:T(128)}, f32[384,32]{0,1:T(8,128)S(1)}, f32[384,32]{0,1:T(8,128)S(1)}, f32[384,32,128]{2,0,1:T(8,128)}, s32[384]{0:T(512)S(1)}, /*index=5*/s...) while((s32[]{:T(128)}, f32[384,32]{0,1:T(8,128)S(1)}, ...), condition=%wide.region_9.10_spmd, body=%wide.region_3.9_spmd.sunk | while | flops 1674141696 | bytes 104477920 | solution.py:85
  92.0 0.8 fusion.31
  93.4 19.2 %conditional.2 = ((f32[384,32]{0,1:T(8,128)S(1)}, f32[384,32]{0,1:T(8,128)S(1)}, f32[384,32,128]{2,0,1:T(8,128)})) conditional(s32[]{:T(128)} %convert_element_type.41, (f32[384,32]{0,1:T(8,128)S(1)}, f32[384,32]{0,1:T(8,128)S(1)}, f32[384,32,128]{2,0,1:T(8,128)}) %tuple.50, (pred[384,256]{0,1:T(8,128)(4,1)S(1)}, bf16[2,256,32,128]{3,1,2,0:T(8,128)(2,1)}, ...), branch_computations={%region_5.5_spmd, %region_6.8_spmd} | conditional | flops 1673748480 | bytes 104370152 | solution.py:62
  93.5 0.0 slice-start
  93.5 0.1 subtract_convert_fusion
  93.6 0.0 slice-start.1
  93.6 4.5 %fusion.3 = (f32[384,32]{0,1:T(8,128)S(1)}, f32[32,256,384]{2,1,0:T(8,128)S(1)}) fusion(f32[384,256]{0,1:T(8,128)S(1)} %subtract_convert_fusion, f32[32]{0:T(128)S(1)} %get-tuple-element.141, pred[384,256]{0,1:T(8,128)(4,1)S(1)} %get-tuple-element.137, bf16[384,32,128]{2,0,1:T(8,128)(2,1)S(1)} %get-tuple-element.140, ...), kind=kOutput, calls=%fused_computation.5 | convolution fusion | flops 821022720 | bytes 18367104 | tf_op jit(solution)/shard_map/while/body/eval_jaxpr/cond/branch_1_fun/qhd,khd->qhk/dot_general | solution.py:39
  98.1 4.3 %fusion.2 = f32[384,32]{0,1:T(8,128)S(1)} fusion(f32[32,256,384]{2,1,0:T(8,128)S(1)} %get-tuple-element.239, f32[384,32]{0,1:T(8,128)S(1)} %max.8, f32[384,256]{0,1:T(8,128)S(1)} %subtract_convert_fusion, f32[32]{0:T(128)S(1)} %get-tuple-element.141, pred[384,256]{0,1:T(8,128)(4,1)S(1)} %get-tuple-element.137), kind=kLoop, calls=%fused_computation.4 | loop fusion | flops 22007808 | bytes 13172864 | tf_op jit(solution)/shard_map/while/body/eval_jaxpr/cond/branch_1_fun/reduce_sum | solution.py:49
  102.5 7.5 %bitcast_add_fusion = f32[384,32,128]{2,0,1:T(8,128)S(1)} fusion(f32[384,32,128]{2,0,1:T(8,128)S(1)} %bitcast.45, f32[384,32]{0,1:T(8,128)S(1)} %get-tuple-element.230, f32[32,256,384]{2,1,0:T(8,128)S(1)} %get-tuple-element.239, f32[384,32]{0,1:T(8,128)S(1)} %max.8, f32[384,256]{0,1:T(8,128)S(1)} %subtract_convert_fusion, f32[32]{0:T(128)S(1)} %get-tuple-element.141, ...), kind=kOutput, calls=%fused_computation.6 | convolution fusion | flops 830472192 | bytes 27853440 | tf_op jit(solution)/shard_map/while/body/eval_jaxpr/cond/branch_1_fun/qhk,khd->qhd/dot_general | solution.py:50
  110.0 2.7 %copy-done = f32[384,32,128]{2,0,1:T(8,128)} copy-done((f32[384,32,128]{2,0,1:T(8,128)}, f32[384,32,128]{2,0,1:T(8,128)S(1)}, u32[]{:S(2)}) %copy-start) | copy-done | bytes 6291480 | tf_op jit(solution)/shard_map/while/body/eval_jaxpr/cond
  112.7 0.8 fusion.31
  114.1 19.2 %conditional.2 = ((f32[384,32]{0,1:T(8,128)S(1)}, f32[384,32]{0,1:T(8,128)S(1)}, f32[384,32,128]{2,0,1:T(8,128)})) conditional(s32[]{:T(128)} %convert_element_type.41, (f32[384,32]{0,1:T(8,128)S(1)}, f32[384,32]{0,1:T(8,128)S(1)}, f32[384,32,128]{2,0,1:T(8,128)}) %tuple.50, (pred[384,256]{0,1:T(8,128)(4,1)S(1)}, bf16[2,256,32,128]{3,1,2,0:T(8,128)(2,1)}, ...), branch_computations={%region_5.5_spmd, %region_6.8_spmd} | conditional | flops 1673748480 | bytes 104370152 | solution.py:62
  114.1 0.1 subtract_convert_fusion
  114.2 0.0 slice-start.1
  114.2 4.5 %fusion.3 = (f32[384,32]{0,1:T(8,128)S(1)}, f32[32,256,384]{2,1,0:T(8,128)S(1)}) fusion(f32[384,256]{0,1:T(8,128)S(1)} %subtract_convert_fusion, f32[32]{0:T(128)S(1)} %get-tuple-element.141, pred[384,256]{0,1:T(8,128)(4,1)S(1)} %get-tuple-element.137, bf16[384,32,128]{2,0,1:T(8,128)(2,1)S(1)} %get-tuple-element.140, ...), kind=kOutput, calls=%fused_computation.5 | convolution fusion | flops 821022720 | bytes 18367104 | tf_op jit(solution)/shard_map/while/body/eval_jaxpr/cond/branch_1_fun/qhd,khd->qhk/dot_general | solution.py:39
  118.8 4.3 %fusion.2 = f32[384,32]{0,1:T(8,128)S(1)} fusion(f32[32,256,384]{2,1,0:T(8,128)S(1)} %get-tuple-element.239, f32[384,32]{0,1:T(8,128)S(1)} %max.8, f32[384,256]{0,1:T(8,128)S(1)} %subtract_convert_fusion, f32[32]{0:T(128)S(1)} %get-tuple-element.141, pred[384,256]{0,1:T(8,128)(4,1)S(1)} %get-tuple-element.137), kind=kLoop, calls=%fused_computation.4 | loop fusion | flops 22007808 | bytes 13172864 | tf_op jit(solution)/shard_map/while/body/eval_jaxpr/cond/branch_1_fun/reduce_sum | solution.py:49
  123.1 7.5 %bitcast_add_fusion = f32[384,32,128]{2,0,1:T(8,128)S(1)} fusion(f32[384,32,128]{2,0,1:T(8,128)S(1)} %bitcast.45, f32[384,32]{0,1:T(8,128)S(1)} %get-tuple-element.230, f32[32,256,384]{2,1,0:T(8,128)S(1)} %get-tuple-element.239, f32[384,32]{0,1:T(8,128)S(1)} %max.8, f32[384,256]{0,1:T(8,128)S(1)} %subtract_convert_fusion, f32[32]{0:T(128)S(1)} %get-tuple-element.141, ...), kind=kOutput, calls=%fused_computation.6 | convolution fusion | flops 830472192 | bytes 27853440 | tf_op jit(solution)/shard_map/while/body/eval_jaxpr/cond/branch_1_fun/qhk,khd->qhd/dot_general | solution.py:50
  130.6 2.7 %copy-done = f32[384,32,128]{2,0,1:T(8,128)} copy-done((f32[384,32,128]{2,0,1:T(8,128)}, f32[384,32,128]{2,0,1:T(8,128)S(1)}, u32[]{:S(2)}) %copy-start) | copy-done | bytes 6291480 | tf_op jit(solution)/shard_map/while/body/eval_jaxpr/cond
  133.3 2.5 fusion.25
  135.8 1.4 collective-permute-start.4
  137.2 5.5 %collective-permute-start.7 = (f32[128,32,128]{2,0,1:T(8,128)S(1)}, f32[128,32,128]{2,0,1:T(8,128)S(1)}, u32[]{:S(2)}, u32[]{:S(2)}) collective-permute-start(f32[128,32,128]{2,0,1:T(8,128)S(1)} %get-tuple-element.243), channel_id=1, source_target_pairs={{0,8},{4,12},{8,16},{12,20},{16,24},{20,28},{1,9},{5,13},{9,17},{1... | collective-permute-start | bytes 6291464 | tf_op jit(solution)/shard_map/ppermute | solution.py:17
  142.7 3.4 %collective-permute-start.2 = (f32[128,32]{0,1:T(8,128)S(1)}, f32[128,32]{0,1:T(8,128)S(1)}, u32[]{:S(2)}, u32[]{:S(2)}) collective-permute-start(f32[128,32]{0,1:T(8,128)S(1)} %get-tuple-element.246), channel_id=1, source_target_pairs={{0,4},{4,8},{8,12},{12,16},{16,20},{20,24},{24,28},{1,5},{5,9},{9,... | collective-permute-start | bytes 49160 | tf_op jit(solution)/shard_map/ppermute | solution.py:17
  146.1 3.3 %collective-permute-start.3 = (f32[128,32]{0,1:T(8,128)S(1)}, f32[128,32]{0,1:T(8,128)S(1)}, u32[]{:S(2)}, u32[]{:S(2)}) collective-permute-start(f32[128,32]{0,1:T(8,128)S(1)} %get-tuple-element.245), channel_id=1, source_target_pairs={{0,4},{4,8},{8,12},{12,16},{16,20},{20,24},{24,28},{1,5},{5,9},{9,... | collective-permute-start | bytes 49160 | tf_op jit(solution)/shard_map/ppermute | solution.py:17
  149.4 1.9 collective-permute-start.5
  151.3 31.9 %collective-permute-done.2 = f32[128,32]{0,1:T(8,128)S(1)} collective-permute-done((f32[128,32]{0,1:T(8,128)S(1)}, f32[128,32]{0,1:T(8,128)S(1)}, u32[]{:S(2)}, u32[]{:S(2)}) %collective-permute-start.2) | collective-permute-done | bytes 16416 | tf_op jit(solution)/shard_map/ppermute | solution.py:17
  183.2 52.2 %collective-permute-start.6 = (f32[128,32]{0,1:T(8,128)S(1)}, f32[128,32]{0,1:T(8,128)S(1)}, u32[]{:S(2)}, u32[]{:S(2)}) collective-permute-start(f32[128,32]{0,1:T(8,128)S(1)} %get-tuple-element.244), channel_id=1, source_target_pairs={{0,8},{4,12},{8,16},{12,20},{16,24},{20,28},{1,9},{5,13},{9,17},{1... | collective-permute-start | bytes 49160 | tf_op jit(solution)/shard_map/ppermute | solution.py:17
  235.4 1.4 collective-permute-done.6
  236.9 7.0 %copy_bitcast_fusion = bf16[128,4096]{1,0:T(8,128)(2,1)} fusion(f32[128,32]{0,1:T(8,128)S(1)} %get-tuple-element.233, f32[128,32,128]{2,0,1:T(8,128)S(1)} %collective-permute-done.7, f32[128,32]{0,1:T(8,128)S(1)} %get-tuple-element.237, f32[128,32]{0,1:T(8,128)S(1)} %get-tuple-element.236, f32[128,32,128]{2,0,1:T(8,128)S(1)} %collective-permute-done.4, ...), kind=kLoop, calls=%fused_computation.27 | loop fusion | flops 4194304 | bytes 7421952 | tf_op jit(solution)/shard_map/reshape | solution.py:167
  (45 shorter events, 0.2 us)
Async XLA Ops:
  6.5 5.1 %copy-start.3 = (bf16[128,4096]{1,0:T(8,128)(2,1)S(1)}, bf16[128,4096]{1,0:T(8,128)(2,1)}, u32[]{:S(2)}) copy-start(bf16[128,4096]{1,0:T(8,128)(2,1)} %param.9) | copy-start | bytes 3145732
  6.5 8.4 %copy-start.6 = (s32[8]{0:T(128)S(1)}, s32[8]{0:T(128)}, u32[]{:S(2)}) copy-start(s32[8]{0:T(128)} %param.12) | copy-start | bytes 100
  6.5 62.8 %all-gather.3.cloned.1.call-start = ((), (), s32[]{:S(2)}) async-start(), calls=%async_computation | async-start | bytes 5242880 | tf_op jit(solution)/shard_map/all_gather | solution.py:155
  9.1 73.4 %all-gather.5.cloned.1.call-start = ((), (), s32[]{:S(2)}) async-start(), calls=%async_computation.1 | async-start | bytes 5242880 | tf_op jit(solution)/shard_map/all_gather | solution.py:158
  12.3 28.0 %copy-start.1 = (bf16[128,4096]{0,1:T(8,128)(2,1)}, bf16[128,4096]{0,1:T(8,128)(2,1)S(1)}, u32[]{:S(2)}) copy-start(bf16[128,4096]{0,1:T(8,128)(2,1)S(1)} %copy.21) | copy-start | bytes 3145732
  12.3 28.0 %collective-permute-start = (bf16[128,32,128]{0,2,1:T(8,128)(2,1)S(1)}, bf16[128,32,128]{0,2,1:T(8,128)(2,1)S(1)}, u32[]{:S(2)}, u32[]{:S(2)}) collective-permute-start(bf16[128,32,128]{0,2,1:T(8,128)(2,1)S(1)} %bitcast.50), channel_id=1, source_target_pairs={{4,0},{8,4},{12,8},{16,12},{20,16},{24,20},{28,24},{5,1},{9,5},{13... | collective-permute-start | bytes 3145736 | tf_op jit(solution)/shard_map/ppermute | solution.py:17
  13.6 50.5 %collective-permute-start.1 = (bf16[128,32,128]{0,2,1:T(8,128)(2,1)S(1)}, bf16[128,32,128]{0,2,1:T(8,128)(2,1)}, u32[]{:S(2)}, u32[]{:S(2)}) collective-permute-start(bf16[128,32,128]{0,2,1:T(8,128)(2,1)S(1)} %bitcast.51), channel_id=1, source_target_pairs={{8,0},{12,4},{16,8},{20,12},{24,16},{28,20},{9,1},{13,5},{17,9},{2... | collective-permute-start | bytes 3145736 | tf_op jit(solution)/shard_map/ppermute | solution.py:17
  40.3 1.0 copy-start.4
  82.5 9.5 %copy-start.2 = (bf16[384,32,128]{2,0,1:T(8,128)(2,1)S(1)}, bf16[384,32,128]{2,0,1:T(8,128)(2,1)}, u32[]{:S(2)}) copy-start(bf16[384,32,128]{2,0,1:T(8,128)(2,1)} %copy.23) | copy-start | bytes 9437188
  82.5 9.5 %copy-start.5 = (f32[32]{0:T(128)S(1)}, f32[32]{0:T(128)}, u32[]{:S(2)}) copy-start(f32[32]{0:T(128)} %param.13) | copy-start | bytes 388
  93.5 9.0 %slice-start = ((s8[6291456]{0:T(1024)(128)(4,1)}), s8[4194304]{0:T(1024)(128)(4,1)S(1)}, s32[]{:S(2)}) async-start(s8[6291456]{0:T(1024)(128)(4,1)} %bitcast.44), calls=%async_computation.2 | async-start | bytes 8388608 | tf_op jit(solution)/shard_map/while/body/eval_jaxpr/cond
  93.6 8.9 %slice-start.1 = ((s8[6291456]{0:T(1024)(128)(4,1)}), s8[2097152]{0:T(1024)(128)(4,1)S(1)}, s32[]{:S(2)}) async-start(s8[6291456]{0:T(1024)(128)(4,1)} %bitcast.44), calls=%async_computation.3 | async-start | bytes 4194304 | tf_op jit(solution)/shard_map/while/body/eval_jaxpr/cond
  110.0 2.7 %copy-start = (f32[384,32,128]{2,0,1:T(8,128)}, f32[384,32,128]{2,0,1:T(8,128)S(1)}, u32[]{:S(2)}) copy-start(f32[384,32,128]{2,0,1:T(8,128)S(1)} %bitcast_add_fusion) | copy-start | bytes 18874372 | tf_op jit(solution)/shard_map/while/body/eval_jaxpr/cond
  114.1 9.0 %slice-start = ((s8[6291456]{0:T(1024)(128)(4,1)}), s8[4194304]{0:T(1024)(128)(4,1)S(1)}, s32[]{:S(2)}) async-start(s8[6291456]{0:T(1024)(128)(4,1)} %bitcast.44), calls=%async_computation.2 | async-start | bytes 8388608 | tf_op jit(solution)/shard_map/while/body/eval_jaxpr/cond
  114.2 8.9 %slice-start.1 = ((s8[6291456]{0:T(1024)(128)(4,1)}), s8[2097152]{0:T(1024)(128)(4,1)S(1)}, s32[]{:S(2)}) async-start(s8[6291456]{0:T(1024)(128)(4,1)} %bitcast.44), calls=%async_computation.3 | async-start | bytes 4194304 | tf_op jit(solution)/shard_map/while/body/eval_jaxpr/cond
  130.6 2.7 %copy-start = (f32[384,32,128]{2,0,1:T(8,128)}, f32[384,32,128]{2,0,1:T(8,128)S(1)}, u32[]{:S(2)}) copy-start(f32[384,32,128]{2,0,1:T(8,128)S(1)} %bitcast_add_fusion) | copy-start | bytes 18874372 | tf_op jit(solution)/shard_map/while/body/eval_jaxpr/cond
  135.8 101.1 %collective-permute-start.4 = (f32[128,32,128]{2,0,1:T(8,128)S(1)}, f32[128,32,128]{2,0,1:T(8,128)S(1)}, u32[]{:S(2)}, u32[]{:S(2)}) collective-permute-start(f32[128,32,128]{2,0,1:T(8,128)S(1)} %get-tuple-element.242), channel_id=1, source_target_pairs={{0,4},{4,8},{8,12},{12,16},{16,20},{20,24},{24,28},{1,5},{5,9},{9,... | collective-permute-start | bytes 6291464 | tf_op jit(solution)/shard_map/ppermute | solution.py:17
  137.2 99.6 %collective-permute-start.7 = (f32[128,32,128]{2,0,1:T(8,128)S(1)}, f32[128,32,128]{2,0,1:T(8,128)S(1)}, u32[]{:S(2)}, u32[]{:S(2)}) collective-permute-start(f32[128,32,128]{2,0,1:T(8,128)S(1)} %get-tuple-element.243), channel_id=1, source_target_pairs={{0,8},{4,12},{8,16},{12,20},{16,24},{20,28},{1,9},{5,13},{9,17},{1... | collective-permute-start | bytes 6291464 | tf_op jit(solution)/shard_map/ppermute | solution.py:17
  142.7 40.5 %collective-permute-start.2 = (f32[128,32]{0,1:T(8,128)S(1)}, f32[128,32]{0,1:T(8,128)S(1)}, u32[]{:S(2)}, u32[]{:S(2)}) collective-permute-start(f32[128,32]{0,1:T(8,128)S(1)} %get-tuple-element.246), channel_id=1, source_target_pairs={{0,4},{4,8},{8,12},{12,16},{16,20},{20,24},{24,28},{1,5},{5,9},{9,... | collective-permute-start | bytes 49160 | tf_op jit(solution)/shard_map/ppermute | solution.py:17
  146.1 89.3 %collective-permute-start.3 = (f32[128,32]{0,1:T(8,128)S(1)}, f32[128,32]{0,1:T(8,128)S(1)}, u32[]{:S(2)}, u32[]{:S(2)}) collective-permute-start(f32[128,32]{0,1:T(8,128)S(1)} %get-tuple-element.245), channel_id=1, source_target_pairs={{0,4},{4,8},{8,12},{12,16},{16,20},{20,24},{24,28},{1,5},{5,9},{9,... | collective-permute-start | bytes 49160 | tf_op jit(solution)/shard_map/ppermute | solution.py:17
  149.4 86.0 %collective-permute-start.5 = (f32[128,32]{0,1:T(8,128)S(1)}, f32[128,32]{0,1:T(8,128)S(1)}, u32[]{:S(2)}, u32[]{:S(2)}) collective-permute-start(f32[128,32]{0,1:T(8,128)S(1)} %get-tuple-element.247), channel_id=1, source_target_pairs={{0,8},{4,12},{8,16},{12,20},{16,24},{20,28},{1,9},{5,13},{9,17},{1... | collective-permute-start | bytes 49160 | tf_op jit(solution)/shard_map/ppermute | solution.py:17
  183.2 53.6 %collective-permute-start.6 = (f32[128,32]{0,1:T(8,128)S(1)}, f32[128,32]{0,1:T(8,128)S(1)}, u32[]{:S(2)}, u32[]{:S(2)}) collective-permute-start(f32[128,32]{0,1:T(8,128)S(1)} %get-tuple-element.244), channel_id=1, source_target_pairs={{0,8},{4,12},{8,16},{12,20},{16,24},{20,28},{1,9},{5,13},{9,17},{1... | collective-permute-start | bytes 49160 | tf_op jit(solution)/shard_map/ppermute | solution.py:17
Sparse Core Ops, SparseCore 0:
  9.2 37.1 all-gather.2
  48.0 34.4 all-gather.4
where the time goes:
time: 251 us
  waiting for transfers between devices  88.3 us (35%)
  starting transfers between devices  70.3 us (28%)
  local copies, waits for them, and re-layouts  32.8 us (13%)
  matrix products  24 us (10%)
  other arithmetic  20.2 us (8%)
  between operations  13.6 us (5%)
    ppermute x8, waiting for transfers between devices, shifted(): lax.ppermute(value, axis, [(source, source + steps) for source in range(f...  81 us
    ppermute x8, starting transfers between devices, shifted(): lax.ppermute(value, axis, [(source, source + steps) for source in range(f...  70.3 us
    dot_general x2, matrix products, update(): jnp.einsum('qhk,khd->qhd', weights.astype(jnp.bfloat16), value_slab, pref...  15 us
    while x3, local copies, waits for them, and re-layouts, attend_keys(): result, unused = lax.scan(scan_step, status, stacked)  14.8 us
    dot_general x2, matrix products, update(): jnp.einsum('qhd,khd->qhk', query_rows, key_slab, preferred_element_type=j...  9.02 us
    reduce_sum x2, other arithmetic, update(): row_total = row_total * rescale + jnp.sum(weights, axis=-1)  8.57 us
    all_gather x1, waiting for transfers between devices, per_device(): lax.all_gather(value_states.reshape(rows_dev, head_count, head_width), 'i...  7.25 us
    reshape x1, other arithmetic, per_device(): return normalize(combined).reshape(rows_dev, head_count * head_width)  6.98 us
  transfers between devices with their start and end apart: 10, of which 5 were waited for; matrix products, arithmetic and copies ran while one was open for 6% of the time, Pallas kernels for 0%

commit v1 on v0

v1 whole, which is shorter than its diff:
```python
import functools
import math

import jax
import jax.numpy as jnp
from jax import lax
from jax.experimental import pallas as pl
from jax.experimental.pallas import tpu as pltpu
from jax.sharding import PartitionSpec as P

DOC_MAX = 1024
BLOCK = 256
NEG_FILL = -1e30
LOG2E = math.log2(math.e)
MESH = pl.DeviceIdType.MESH


def kernel(
    plane_groups, inner_count, planes, heads, width,
    doc_ref, slope_ref, q_ref, k_ref, v_ref, out_ref,
    q_buf, k_buf, v_buf, o_buf, start_buf,
    in_send, in_recv, z_send, z_recv, out_send, out_recv,
):
    rows = q_ref.shape[0]
    slots = plane_groups * inner_count
    outer = lax.axis_index("outer")
    inner = lax.axis_index("inner")
    plane = outer // plane_groups
    slot = (outer % plane_groups) * inner_count + inner
    has_prev = plane > 0
    has_next = plane < planes - 1
    prev_id = {"outer": outer - plane_groups, "inner": inner}
    next_id = {"outer": outer + plane_groups, "inner": inner}

    def peer_of(step):
        peer = (slot + step) % slots
        return peer, {"outer": plane * plane_groups + peer // inner_count, "inner": peer % inner_count}

    def columns(owner, head):
        return pl.ds(pl.multiple_of((owner * heads + head) * width, width), width)

    own_rows = pl.ds(pl.multiple_of(slot * rows, rows), rows)
    home_rows = pl.ds(pl.multiple_of(DOC_MAX + slot * rows, rows), rows)

    barrier = pltpu.get_barrier_semaphore()
    for step in range(1, slots):
        pl.semaphore_signal(barrier, inc=1, device_id=peer_of(step)[1], device_id_type=MESH)

    @pl.when(has_prev)
    def _():
        pl.semaphore_signal(barrier, inc=1, device_id=prev_id, device_id_type=MESH)

    @pl.when(has_next)
    def _():
        pl.semaphore_signal(barrier, inc=1, device_id=next_id, device_id_type=MESH)

    pl.semaphore_wait(barrier, slots - 1 + has_prev.astype(jnp.int32) + has_next.astype(jnp.int32))

    tensors = ((k_ref, k_buf, home_rows), (v_ref, v_buf, home_rows), (q_ref, q_buf, own_rows))
    for head in range(heads):
        for kind, (source, target, place) in enumerate(tensors):
            for step in range(1, slots):
                peer, peer_id = peer_of(step)
                pltpu.make_async_remote_copy(
                    src_ref=source.at[:, columns(peer, head)],
                    dst_ref=target.at[head, place, :],
                    send_sem=in_send.at[kind],
                    recv_sem=in_recv.at[kind, head],
                    device_id=peer_id,
                    device_id_type=MESH,
                ).start()
            pltpu.make_async_copy(
                source.at[:, columns(slot, head)], target.at[head, place, :], in_recv.at[kind, head]
            ).start()

    @pl.when(jnp.logical_not(has_prev))
    def _():
        k_buf[:, :DOC_MAX, :] = jnp.zeros((heads, DOC_MAX, width), k_buf.dtype)
        v_buf[:, :DOC_MAX, :] = jnp.zeros((heads, DOC_MAX, width), v_buf.dtype)

    position = plane * DOC_MAX + lax.broadcasted_iota(jnp.int32, (DOC_MAX, 1), 0)

    def next_document(index, carry):
        end, start = carry
        end = end + doc_ref[index]
        return end, jnp.where(position >= end, end, start)

    start = lax.fori_loop(
        0, doc_ref.shape[0], next_document, (jnp.int32(0), jnp.zeros((DOC_MAX, 1), jnp.int32))
    )[1]
    start_buf[...] = (start - (plane - 1) * DOC_MAX).astype(jnp.float32)

    def whole(ref, sem):
        return pltpu.make_async_copy(ref, ref, sem)

    def forward(head):
        for kind, buf in enumerate((k_buf, v_buf)):
            whole(buf.at[head, pl.ds(DOC_MAX, DOC_MAX), :], in_recv.at[kind, head]).wait()

            @pl.when(has_next)
            def _():
                pltpu.make_async_remote_copy(
                    src_ref=buf.at[head, pl.ds(DOC_MAX, DOC_MAX), :],
                    dst_ref=buf.at[head, pl.ds(0, DOC_MAX), :],
                    send_sem=z_send.at[kind, head],
                    recv_sem=z_recv.at[kind, head],
                    device_id=next_id,
                    device_id_type=MESH,
                ).start()

    window = DOC_MAX + BLOCK

    def attend(head):
        whole(q_buf.at[head], in_recv.at[2, head]).wait()

        @pl.when(has_prev)
        def _():
            for kind, buf in enumerate((k_buf, v_buf)):
                whole(buf.at[head, pl.ds(0, DOC_MAX), :], z_recv.at[kind, head]).wait()

        slope = slope_ref[slot * heads + head] * LOG2E
        scale = LOG2E / math.sqrt(width)

        def one_block(index, unused):
            first = pl.multiple_of(index * BLOCK, BLOCK)
            query = q_buf[head, pl.ds(first, BLOCK), :]
            keys = k_buf[head, pl.ds(first, window), :]
            values = v_buf[head, pl.ds(first, window), :]
            scores = lax.dot_general(
                query, keys, (((1,), (1,)), ((), ())), preferred_element_type=jnp.float32
            )
            key_pos = lax.broadcasted_iota(jnp.int32, (1, window), 1).astype(jnp.float32)
            query_pos = (lax.broadcasted_iota(jnp.int32, (BLOCK, 1), 0) + DOC_MAX).astype(jnp.float32)
            earliest = start_buf[pl.ds(first, BLOCK), :] - first.astype(jnp.float32)
            allowed = (key_pos >= earliest) & (key_pos <= query_pos)
            scores = jnp.where(allowed, scores * scale + slope * key_pos, NEG_FILL)
            row_max = jnp.max(scores, axis=1, keepdims=True)
            weights = jnp.exp2(scores - row_max)
            row_total = jnp.sum(weights, axis=1, keepdims=True)
            numerator = jnp.dot(
                weights.astype(jnp.bfloat16), values, preferred_element_type=jnp.float32
            )
            o_buf[head, pl.ds(first, BLOCK), :] = (numerator / row_total).astype(o_buf.dtype)
            return unused

        lax.fori_loop(0, DOC_MAX // BLOCK, one_block, 0)
        for step in range(1, slots):
            peer, peer_id = peer_of(step)
            pltpu.make_async_remote_copy(
                src_ref=o_buf.at[head, pl.ds(pl.multiple_of(peer * rows, rows), rows), :],
                dst_ref=out_ref.at[:, columns(slot, head)],
                send_sem=out_send,
                recv_sem=out_recv,
                device_id=peer_id,
                device_id_type=MESH,
            ).start()
        pltpu.make_async_copy(
            o_buf.at[head, own_rows, :], out_ref.at[:, columns(slot, head)], out_recv
        ).start()

    forward(0)
    for head in range(1, heads):
        forward(head)
        attend(head - 1)
    attend(heads - 1)

    sent = pl.ds(0, (slots - 1) * heads * width)
    for kind, (source, unused, place) in enumerate(tensors):
        whole(source.at[:, sent], in_send.at[kind]).wait()
    whole(out_ref.at[:, sent], out_send).wait()

    @pl.when(has_next)
    def _():
        for head in range(heads):
            for kind, buf in enumerate((k_buf, v_buf)):
                whole(buf.at[head, pl.ds(DOC_MAX, DOC_MAX), :], z_send.at[kind, head]).wait()

    whole(out_ref, out_recv).wait()


def per_device(query_states, key_states, value_states, doc_lengths, slopes):
    rows, all_columns = query_states.shape
    width = all_columns // slopes.shape[0]
    inner_count = lax.axis_size("inner")
    plane_groups = DOC_MAX // (rows * inner_count)
    slots = plane_groups * inner_count
    planes = lax.axis_size("outer") // plane_groups
    heads = slopes.shape[0] // slots
    dtype = query_states.dtype
    return pl.pallas_call(
        functools.partial(kernel, plane_groups, inner_count, planes, heads, width),
        out_shape=jax.ShapeDtypeStruct((rows, all_columns), dtype),
        in_specs=[pl.BlockSpec(memory_space=pltpu.SMEM)] * 2 + [pl.BlockSpec(memory_space=pl.ANY)] * 3,
        out_specs=pl.BlockSpec(memory_space=pl.ANY),
        scratch_shapes=[
            pltpu.VMEM((heads, DOC_MAX, width), dtype),
            pltpu.VMEM((heads, 2 * DOC_MAX, width), dtype),
            pltpu.VMEM((heads, 2 * DOC_MAX, width), dtype),
            pltpu.VMEM((heads, DOC_MAX, width), dtype),
            pltpu.VMEM((DOC_MAX, 1), jnp.float32),
            pltpu.SemaphoreType.DMA((3,)),
            pltpu.SemaphoreType.DMA((3, heads)),
            pltpu.SemaphoreType.DMA((2, heads)),
            pltpu.SemaphoreType.DMA((2, heads)),
            pltpu.SemaphoreType.DMA,
            pltpu.SemaphoreType.DMA,
        ],
        compiler_params=pltpu.CompilerParams(
            collective_id=0, has_side_effects=True, vmem_limit_bytes=48 * 1024 * 1024
        ),
        cost_estimate=pl.CostEstimate(
            flops=4 * heads * DOC_MAX * (DOC_MAX + BLOCK) * width,
            bytes_accessed=8 * rows * all_columns,
            transcendentals=heads * DOC_MAX * (DOC_MAX + BLOCK),
        ),
    )(doc_lengths, slopes, query_states, key_states, value_states)


def solution(mesh):
    placed = P(("outer", "inner"), None)
    return jax.shard_map(
        per_device,
        mesh=mesh,
        in_specs=(placed, placed, placed, P(), P()),
        out_specs=placed,
        check_vma=False,
    )
```

time: 251 us -> 69.6 us (0.28)
  the two profiles are of different devices: /device:TPU:0 before, /device:TPU:31 now
where the time goes in v1:
time: 69.6 us; the launch traced here: 68.3 us
  Pallas kernels  62.4 us (90%)
  local copies, waits for them, and re-layouts  5.95 us (9%)
    pallas_call x1, Pallas kernels, per_device(): pl.pallas_call(functools.partial(kernel, plane_groups, inner_count, plane...  62.4 us
    unnamed x11, local copies, waits for them, and re-layouts  5.95 us

profile of v1, /device:TPU:31, one launch (start us, length us, event | category | flops | bytes accessed | tf_op | source)
XLA Modules:
  0.0 68.3 jit_solution(13789967216700956069)
XLA Ops:
  0.0 0.0 copy-start
  0.0 1.2 %copy-done = bf16[128,4096]{1,0:T(8,128)(2,1)S(1)} copy-done((bf16[128,4096]{1,0:T(8,128)(2,1)S(1)}, bf16[128,4096]{1,0:T(8,128)(2,1)}, u32[]{:S(2)}) %copy-start) | copy-done | bytes 1048600
  1.2 0.0 copy-start.1
  1.2 1.2 %copy-done.1 = bf16[128,4096]{1,0:T(8,128)(2,1)S(1)} copy-done((bf16[128,4096]{1,0:T(8,128)(2,1)S(1)}, bf16[128,4096]{1,0:T(8,128)(2,1)}, u32[]{:S(2)}) %copy-start.1) | copy-done | bytes 1048600
  2.5 0.0 copy-start.2
  2.5 1.2 %copy-done.2 = bf16[128,4096]{1,0:T(8,128)(2,1)S(1)} copy-done((bf16[128,4096]{1,0:T(8,128)(2,1)S(1)}, bf16[128,4096]{1,0:T(8,128)(2,1)}, u32[]{:S(2)}) %copy-start.2) | copy-done | bytes 1048600
  3.7 0.0 copy-start.3
  3.7 0.7 copy-done.3
  4.3 0.0 copy-start.4
  4.3 0.7 copy-done.4
  5.0 62.4 %shard_map.55 = bf16[128,4096]{1,0:T(8,128)(2,1)S(1)} custom-call(s32[8]{0:T(128)S(1)} %copy-done.3, f32[32]{0:T(128)S(1)} %copy-done.4, bf16[128,4096]{1,0:T(8,128)(2,1)S(1)} %copy-done, bf16[128,4096]{1,0:T(8,128)(2,1)S(1)} %copy-done.1, bf16[128,4096]{1,0:T(8,128)(2,1)S(1)} %copy-done.2), custom_call_target="tpu_custom_call" | custom-call | flops 2684354560 | bytes 4194304 | tf_op jit(solution)/shard_map/pallas_call | solution.py:190
  67.4 1.0 %copy.7 = bf16[128,4096]{1,0:T(8,128)(2,1)} copy(bf16[128,4096]{1,0:T(8,128)(2,1)S(1)} %shard_map.55) | data formatting | bytes 2097152
Async XLA Ops:
  0.0 1.2 %copy-start = (bf16[128,4096]{1,0:T(8,128)(2,1)S(1)}, bf16[128,4096]{1,0:T(8,128)(2,1)}, u32[]{:S(2)}) copy-start(bf16[128,4096]{1,0:T(8,128)(2,1)} %q_ref.1) | copy-start | bytes 3145732
  1.2 1.2 %copy-start.1 = (bf16[128,4096]{1,0:T(8,128)(2,1)S(1)}, bf16[128,4096]{1,0:T(8,128)(2,1)}, u32[]{:S(2)}) copy-start(bf16[128,4096]{1,0:T(8,128)(2,1)} %k_ref.1) | copy-start | bytes 3145732
  2.5 1.2 %copy-start.2 = (bf16[128,4096]{1,0:T(8,128)(2,1)S(1)}, bf16[128,4096]{1,0:T(8,128)(2,1)}, u32[]{:S(2)}) copy-start(bf16[128,4096]{1,0:T(8,128)(2,1)} %v_ref.1) | copy-start | bytes 3145732
  3.7 0.7 copy-start.3
  4.3 0.7 copy-start.4

commit v2 on v1

--- a/solution.py
+++ b/solution.py
@@ -17,9 +17,9 @@
 
 def kernel(
     plane_groups, inner_count, planes, heads, width,
-    doc_ref, slope_ref, q_ref, k_ref, v_ref, out_ref,
-    q_buf, k_buf, v_buf, o_buf, start_buf,
-    in_send, in_recv, z_send, z_recv, out_send, out_recv,
+    doc_hbm, slope_hbm, q_ref, k_ref, v_ref, out_ref,
+    doc_ref, slope_ref, q_buf, k_buf, v_buf, o_buf, start_buf,
+    small_sem, in_send, in_recv, z_send, z_recv, out_send, out_recv,
 ):
     rows = q_ref.shape[0]
     slots = plane_groups * inner_count
@@ -41,6 +41,13 @@
 
     own_rows = pl.ds(pl.multiple_of(slot * rows, rows), rows)
     home_rows = pl.ds(pl.multiple_of(DOC_MAX + slot * rows, rows), rows)
+
+    small = [
+        pltpu.make_async_copy(doc_hbm, doc_ref, small_sem.at[0]),
+        pltpu.make_async_copy(slope_hbm, slope_ref, small_sem.at[1]),
+    ]
+    for copy in small:
+        copy.start()
 
     barrier = pltpu.get_barrier_semaphore()
     for step in range(1, slots):
@@ -77,6 +84,9 @@
     def _():
         k_buf[:, :DOC_MAX, :] = jnp.zeros((heads, DOC_MAX, width), k_buf.dtype)
         v_buf[:, :DOC_MAX, :] = jnp.zeros((heads, DOC_MAX, width), v_buf.dtype)
+
+    for copy in small:
+        copy.wait()
 
     position = plane * DOC_MAX + lax.broadcasted_iota(jnp.int32, (DOC_MAX, 1), 0)
 
@@ -141,22 +151,34 @@
                 weights.astype(jnp.bfloat16), values, preferred_element_type=jnp.float32
             )
             o_buf[head, pl.ds(first, BLOCK), :] = (numerator / row_total).astype(o_buf.dtype)
+
+            for part in range(BLOCK // rows):
+                peer = index * (BLOCK // rows) + part
+                done_rows = o_buf.at[head, pl.ds(pl.multiple_of(peer * rows, rows), rows), :]
+
+                @pl.when(peer != slot)
+                def _():
+                    pltpu.make_async_remote_copy(
+                        src_ref=done_rows,
+                        dst_ref=out_ref.at[:, columns(slot, head)],
+                        send_sem=out_send,
+                        recv_sem=out_recv,
+                        device_id={
+                            "outer": plane * plane_groups + peer // inner_count,
+                            "inner": peer % inner_count,
+                        },
+                        device_id_type=MESH,
+                    ).start()
+
+                @pl.when(peer == slot)
+                def _():
+                    pltpu.make_async_copy(
+                        done_rows, out_ref.at[:, columns(slot, head)], out_recv
+                    ).start()
+
             return unused
 
         lax.fori_loop(0, DOC_MAX // BLOCK, one_block, 0)
-        for step in range(1, slots):
-            peer, peer_id = peer_of(step)
-            pltpu.make_async_remote_copy(
-                src_ref=o_buf.at[head, pl.ds(pl.multiple_of(peer * rows, rows), rows), :],
-                dst_ref=out_ref.at[:, columns(slot, head)],
-                send_sem=out_send,
-                recv_sem=out_recv,
-                device_id=peer_id,
-                device_id_type=MESH,
-            ).start()
-        pltpu.make_async_copy(
-            o_buf.at[head, own_rows, :], out_ref.at[:, columns(slot, head)], out_recv
-        ).start()
 
     forward(0)
     for head in range(1, heads):
@@ -190,14 +212,17 @@
     return pl.pallas_call(
         functools.partial(kernel, plane_groups, inner_count, planes, heads, width),
         out_shape=jax.ShapeDtypeStruct((rows, all_columns), dtype),
-        in_specs=[pl.BlockSpec(memory_space=pltpu.SMEM)] * 2 + [pl.BlockSpec(memory_space=pl.ANY)] * 3,
-        out_specs=pl.BlockSpec(memory_space=pl.ANY),
+        in_specs=[pl.BlockSpec(memory_space=pltpu.HBM)] * 5,
+        out_specs=pl.BlockSpec(memory_space=pltpu.HBM),
         scratch_shapes=[
+            pltpu.SMEM(doc_lengths.shape, doc_lengths.dtype),
+            pltpu.SMEM(slopes.shape, slopes.dtype),
             pltpu.VMEM((heads, DOC_MAX, width), dtype),
             pltpu.VMEM((heads, 2 * DOC_MAX, width), dtype),
             pltpu.VMEM((heads, 2 * DOC_MAX, width), dtype),
             pltpu.VMEM((heads, DOC_MAX, width), dtype),
             pltpu.VMEM((DOC_MAX, 1), jnp.float32),
+            pltpu.SemaphoreType.DMA((2,)),
             pltpu.SemaphoreType.DMA((3,)),
             pltpu.SemaphoreType.DMA((3, heads)),
             pltpu.SemaphoreType.DMA((2, heads)),
@@ -206,7 +231,7 @@
             pltpu.SemaphoreType.DMA,
         ],
         compiler_params=pltpu.CompilerParams(
-            collective_id=0, has_side_effects=True, vmem_limit_bytes=48 * 1024 * 1024
+            collective_id=0, has_side_effects=True, vmem_limit_bytes=64 * 1024 * 1024
         ),
         cost_estimate=pl.CostEstimate(
             flops=4 * heads * DOC_MAX * (DOC_MAX + BLOCK) * width,

time: 69.6 us -> 64.5 us (0.927); the launches traced: 68.3 us -> 64.3 us
  local copies, waits for them, and re-layouts: 5.95 us -> 2.29 us
    unnamed x11 -> x1, local copies, waits for them, and re-layouts: 5.95 us -> 2.29 us
where the time goes in v2:
time: 64.5 us; the launch traced here: 64.3 us
  Pallas kernels  62 us (96%)
  local copies, waits for them, and re-layouts  2.29 us (4%)
    pallas_call x1, Pallas kernels, per_device(): pl.pallas_call(functools.partial(kernel, plane_groups, inner_count, plane...  62 us
    unnamed x1, local copies, waits for them, and re-layouts  2.29 us

profile of v2, /device:TPU:31, one launch (start us, length us, event | category | flops | bytes accessed | tf_op | source)
XLA Modules:
  0.0 64.3 jit_solution(5554945275926677283)
XLA Ops:
  0.0 62.0 %shard_map.55 = bf16[128,4096]{1,0:T(8,128)(2,1)} custom-call(s32[8]{0:T(128)} %doc_hbm.1, f32[32]{0:T(128)} %slope_hbm.1, bf16[128,4096]{1,0:T(8,128)(2,1)} %q_ref.1, bf16[128,4096]{1,0:T(8,128)(2,1)} %k_ref.1, bf16[128,4096]{1,0:T(8,128)(2,1)} %v_ref.1), custom_call_target="tpu_custom_call" | custom-call | flops 2684354560 | bytes 4194304 | tf_op jit(solution)/shard_map/pallas_call | solution.py:212
  62.0 2.3 %copy.7 = bf16[128,4096]{1,0:T(8,128)(2,1)} copy(bf16[128,4096]{1,0:T(8,128)(2,1)} %shard_map.55) | data formatting | bytes 2097152
